TPU v7x, 32 devices: a whole 2x2x4 slice. The times are simulated.
32 devices in a mesh: subj: 4 (over x, core), obj: 8 (over z, y).
Axes of the slice: x: 2, y: 2, z: 4, core: 2. Of those that a mesh axis runs over, the one named last changes fastest.
Arguments:
- subject_factors: bfloat16 [2048, 512], P(('subj', 'obj')), may hold values from -6 to 6
- object_factors: bfloat16 [4096, 512], P(('obj', 'subj')), may hold values from -6 to 6
- relations: bfloat16 [2, 512, 512], P(None, 'subj', 'obj'), may hold values from -0.01171875 to 0.01171875
- labels: int32 [2, 2048, 4096], P(None, 'subj', 'obj'), may hold values from 0 to 2
Outputs:
- grad_subject: float32 [2048, 512], P(('subj', 'obj'))
- grad_object: float32 [4096, 512], P(('obj', 'subj'))
- grad_relations: float32 [2, 512, 512], P(None, 'subj', 'obj')
- loss_rows: float32 [2048], P(('subj', 'obj'))
All inputs are finite; a program needn't handle non-finite values.
Results may differ from a plain program's by a relative error of at most 0.02.
Values may be sent and summed in bfloat16 or wider, within the bound.
A program may use at most 64 MiB of HBM per device.

v0:
```python
import jax
import jax.numpy as jnp
from jax import lax
from jax.sharding import PartitionSpec as P


def project_left(factors, relation_full):
    return jnp.einsum(
        "ic,kca->ika", factors, relation_full, preferred_element_type=jnp.float32
    ).astype(jnp.bfloat16)


def project_right(factors, relation_full):
    return jnp.einsum(
        "jc,kac->jka", factors, relation_full, preferred_element_type=jnp.float32
    ).astype(jnp.bfloat16)


def body(subject_factors, object_factors, relations, labels):
    row_pieces = lax.all_gather(relations, "subj", axis=1, tiled=True)
    relation_full = lax.all_gather(row_pieces, "obj", axis=2, tiled=True)
    relation_count = relation_full.shape[0]
    rank_width = relation_full.shape[1]
    subject_block = lax.all_gather(subject_factors, "obj", axis=0, tiled=True)
    object_block = lax.all_gather(object_factors, "subj", axis=0, tiled=True)
    left = project_left(subject_block, relation_full)
    right = project_right(object_block, relation_full)
    subject_rows = subject_block.shape[0]
    object_rows = object_block.shape[0]
    object_total = object_rows * lax.axis_size("obj")
    subject_total = subject_rows * lax.axis_size("subj")
    subject_grad = jnp.zeros((subject_rows, rank_width), jnp.float32)
    object_grad = jnp.zeros((object_rows, rank_width), jnp.float32)
    loss_sum = jnp.zeros((subject_rows,), jnp.float32)
    relation_terms = []
    for relation in range(relation_count):
        left_part = left[:, relation]
        scores = jnp.einsum(
            "ia,ja->ij", left_part, object_block, preferred_element_type=jnp.float32
        )
        codes = labels[relation]
        target = (codes == 2).astype(jnp.float32)
        weight = (codes > 0).astype(jnp.float32)
        loss_sum = loss_sum + jnp.sum(weight * (jax.nn.softplus(scores) - target * scores), axis=1)
        residual = (weight * (jax.nn.sigmoid(scores) - target)).astype(jnp.bfloat16)
        subject_grad = subject_grad + jnp.dot(
            residual, right[:, relation], preferred_element_type=jnp.float32
        )
        object_grad = object_grad + jnp.einsum(
            "ij,ia->ja", residual, left_part, preferred_element_type=jnp.float32
        )
        carried = jnp.dot(residual, object_block, preferred_element_type=jnp.float32).astype(
            jnp.bfloat16
        )
        relation_terms.append(
            jnp.einsum("ic,ia->ca", subject_block, carried, preferred_element_type=jnp.float32)
        )
    loss_part = loss_sum / (relation_count * object_total)
    grad_subject, loss_rows = (
        lax.psum_scatter(
            subject_grad.astype(jnp.bfloat16), "obj", scatter_dimension=0, tiled=True
        ).astype(jnp.float32),
        lax.psum_scatter(
            loss_part.astype(jnp.bfloat16), "obj", scatter_dimension=0, tiled=True
        ).astype(jnp.float32),
    )
    grad_object = lax.psum_scatter(
        object_grad.astype(jnp.bfloat16), "subj", scatter_dimension=0, tiled=True
    ).astype(jnp.float32)
    relation_stack = jnp.stack(relation_terms)
    partial_rows = lax.psum_scatter(
        relation_stack.astype(jnp.bfloat16), "subj", scatter_dimension=1, tiled=True
    )
    relation_sum = lax.psum_scatter(partial_rows, "obj", scatter_dimension=2, tiled=True).astype(
        jnp.float32
    )
    return (grad_subject, grad_object, relation_sum / subject_total, loss_rows)


def solution(mesh):
    placed = (
        P(("subj", "obj"), None),
        P(("obj", "subj"), None),
        P(None, "subj", "obj"),
        P(None, "subj", "obj"),
    )
    return jax.shard_map(
        body,
        mesh=mesh,
        in_specs=placed,
        out_specs=(
            P(("subj", "obj"), None),
            P(("obj", "subj"), None),
            P(None, "subj", "obj"),
            P(("subj", "obj")),
        ),
        check_vma=False,
    )
```

profile of v0, /device:TPU:0, one launch (start us, length us, event | category | flops | bytes accessed | tf_op | source)
XLA Modules:
  0.0 260.4 jit_solution(10005289679640493581)
XLA Ops:
  7.2 0.0 all-gather.2.cloned.1.call-start
  7.2 8.4 %all_gather.13 = bf16[2,512,64]{1,2,0:T(8,128)(2,1)} all-gather(bf16[2,128,64]{1,2,0:T(8,128)(2,1)} %param.6), channel_id=1, replica_groups=mesh['subj'=4,'obj'=8] {'subj'}, dimensions={1}, use_global_device_ids=true | all-gather | bytes 163840 | tf_op jit(solution)/shard_map/all_gather | solution.py:20
  15.6 0.0 all-gather.2.cloned.1.call-update
  15.6 0.0 reduce-scatter.13.cloned.1.call-start
  15.6 1.7 fusion.16
  17.4 0.0 copy-start.7
  17.4 0.0 copy-start.8
  17.4 1.3 copy.15
  18.7 0.3 copy.14
  19.1 7.3 %all_gather.15 = bf16[512,512]{1,0:T(8,128)(2,1)S(1)} all-gather(bf16[128,512]{1,0:T(8,128)(2,1)S(1)} %copy-done.7), channel_id=1, replica_groups=mesh['subj'=4,'obj'=8] {'subj'}, dimensions={0}, use_global_device_ids=true | all-gather | bytes 655360 | tf_op jit(solution)/shard_map/all_gather | solution.py:25
  26.4 32.6 %all_gather.12 = bf16[512,512]{1,0:T(8,128)(2,1)S(1)} all-gather(bf16[64,512]{1,0:T(8,128)(2,1)S(1)} %copy-done.8), channel_id=1, replica_groups=mesh['subj'=4,'obj'=8] {'obj'}, dimensions={0}, use_global_device_ids=true | all-gather | bytes 589824 | tf_op jit(solution)/shard_map/all_gather | solution.py:24
  59.0 0.6 all-gather.2.cloned.1.call-done
  59.6 2.0 convolution_convert_fusion.1
  61.6 2.9 %fusion.9 = (f32[512]{0:T(512)S(1)}, pred[1,512,512]{1,2,0:T(8,128)(4,1)S(1)}, pred[1,512,512]{1,2,0:T(8,128)(4,1)S(1)}, f32[512,512]{0,1:T(8,128)S(1)}) fusion(s32[1,512,512]{1,2,0:T(8,128)} %copy.15, bf16[512,512]{1,0:T(8,128)(2,1)S(1)} %all_gather.15, bf16[512,2,512]{2,0,1:T(8,128)(2,1)S(1)} %convolution_convert_fusion.1), kind=kOutput, calls=%fused_computation.19 | convolution fusion | flops 271580672 | bytes 3672064 | tf_op jit(solution)/shard_map/ia,ja->ij/dot_general | solution.py:38
  64.5 0.4 select_convert_fusion
  64.8 2.7 %fusion.3 = bf16[1,512,512]{1,2,0:T(8,128)(2,1)} fusion(bf16[512,512]{1,0:T(8,128)(2,1)} %copy-done.4, bf16[512,512]{0,1:T(8,128)(2,1)S(1)} %select_convert_fusion, bf16[512,512]{1,0:T(8,128)(2,1)S(1)} %all_gather.15), kind=kOutput, calls=%fused_computation.13 | convolution fusion | flops 537395200 | bytes 2097152 | tf_op jit(solution)/shard_map/ic,ia->ca/dot_general | solution.py:56
  67.5 0.0 copy-done
  67.5 1.3 fusion.6
  68.8 0.4 select_convert_fusion.1
  69.2 0.6 copy-done.5
  69.9 1.7 fusion.2
  71.5 1.1 pad_maximum_fusion
  72.7 1.0 copy.12
  73.7 1.2 copy.16
  74.9 0.0 reduce-scatter.13.cloned.1.call-update
  74.9 0.0 reduce-scatter.9.cloned.1.call-start
  75.0 0.4 fusion.13
  75.4 1.3 fusion.1
  76.7 0.0 reduce-scatter.9.cloned.1.call-update
  76.7 0.0 reduce-scatter.7.cloned.1.call-start
  76.8 1.9 convolution_convert_fusion
  78.7 0.5 fusion.10
  79.2 0.0 copy-start.9
  79.2 1.3 fusion
  80.5 0.0 reduce-scatter.7.cloned.1.call-update
  80.5 0.0 reduce-scatter.11.cloned.1.call-start
  80.5 18.6 %reduce-scatter.13.cloned.1.call-done = bf16[128,1024]{1,0:T(8,128)(2,1)} async-done(((bf16[512,1024]{1,0:T(8,128)(2,1)}), bf16[128,1024]{1,0:T(8,128)(2,1)}) %reduce-scatter.13.cloned.1.call-update) | async-done | bytes 262160
  99.1 1.1 reshape.19
  100.2 0.9 copy.13
  101.1 0.0 reduce-scatter.11.cloned.1.call-update
  101.2 0.6 dynamic-slice
  102.4 21.4 %all-reduce = bf16[512]{0:T(512)(128)(2,1)S(1)} all-reduce(bf16[512]{0:T(512)(128)(2,1)S(1)} %multiply_convert_fusion), channel_id=6, replica_groups=mesh['subj'=4,'obj'=8] {'obj'}, use_global_device_ids=true, to_apply=%region_6.7.clone | all-reduce | flops 512 | bytes 2048
  123.8 0.6 dynamic-slice_convert_fusion
  124.4 1.6 convert_element_type.57
  126.0 62.6 %reduce-scatter.7.cloned.1.call-done = bf16[64,512]{1,0:T(8,128)(2,1)} async-done(((bf16[512,512]{1,0:T(8,128)(2,1)}), bf16[64,512]{1,0:T(8,128)(2,1)}) %reduce-scatter.7.cloned.1.call-update) | async-done | bytes 65552 | tf_op jit(solution)/shard_map/reduce_scatter | solution.py:60
  188.6 1.5 convert_element_type.55
  190.1 62.4 %reduce-scatter.11.cloned.1.call-done = bf16[2,128,64]{1,2,0:T(8,128)(2,1)} async-done(((bf16[2,128,512]{1,2,0:T(8,128)(2,1)}), bf16[2,128,64]{1,2,0:T(8,128)(2,1)}) %reduce-scatter.11.cloned.1.call-update) | async-done | bytes 32784 | tf_op jit(solution)/shard_map/reduce_scatter | solution.py:74
  252.5 1.4 convert_multiply_fusion
  (17 shorter events, 0.0 us)
Async XLA Ops:
  7.2 52.4 %all-gather.2.cloned.1.call-start = ((), (), s32[]{:S(2)}) async-start(), calls=%async_computation.4 | async-start | bytes 1179648 | tf_op jit(solution)/shard_map/all_gather | solution.py:21
  15.6 83.5 %reduce-scatter.13.cloned.1.call-start = ((), (), s32[]{:S(2)}) async-start(), calls=%async_computation.8 | async-start | bytes 1310720
  17.4 1.7 copy-start.7
  17.4 9.0 %copy-start.8 = (bf16[64,512]{1,0:T(8,128)(2,1)S(1)}, bf16[64,512]{1,0:T(8,128)(2,1)}, u32[]{:S(2)}) copy-start(bf16[64,512]{1,0:T(8,128)(2,1)} %param.4) | copy-start | bytes 196612
  26.4 42.9 %copy-start.2 = (bf16[512,512]{1,0:T(8,128)(2,1)}, bf16[512,512]{1,0:T(8,128)(2,1)S(1)}, u32[]{:S(2)}) copy-start(bf16[512,512]{1,0:T(8,128)(2,1)S(1)} %all_gather.15) | copy-start | bytes 1572868
  59.0 5.5 %copy-start.4 = (bf16[512,512]{1,0:T(8,128)(2,1)}, bf16[512,512]{1,0:T(8,128)(2,1)S(1)}, u32[]{:S(2)}) copy-start(bf16[512,512]{1,0:T(8,128)(2,1)S(1)} %all_gather.12) | copy-start | bytes 1572868
  61.6 6.0 %copy-start = (bf16[512,2,512]{2,0,1:T(8,128)(2,1)}, bf16[512,2,512]{2,0,1:T(8,128)(2,1)S(1)}, u32[]{:S(2)}) copy-start(bf16[512,2,512]{2,0,1:T(8,128)(2,1)S(1)} %convolution_convert_fusion.1) | copy-start | bytes 3145732
  68.8 1.0 copy-start.5
  68.8 2.7 %copy-start.6 = (bf16[1,512,512]{1,2,0:T(8,128)(2,1)S(1)}, bf16[1,512,512]{1,2,0:T(8,128)(2,1)}, u32[]{:S(2)}) copy-start(bf16[1,512,512]{1,2,0:T(8,128)(2,1)} %fusion.3) | copy-start | bytes 1572868
  73.7 1.3 copy-start.1
  74.9 49.4 %reduce-scatter.9.cloned.1.call-start = ((), (), s32[]{:S(2)}) async-start(), calls=%async_computation.6 | async-start | bytes 655360 | tf_op jit(solution)/shard_map/reduce_scatter | solution.py:67
  75.4 1.3 copy-start.3
  76.7 111.9 %reduce-scatter.7.cloned.1.call-start = ((), (), s32[]{:S(2)}) async-start(), calls=%async_computation.5 | async-start | bytes 589824 | tf_op jit(solution)/shard_map/reduce_scatter | solution.py:60
  79.2 22.0 %copy-start.9 = (u32[32]{0:T(128)S(1)}, u32[32]{0:T(128)}, u32[]{:S(2)}) copy-start(u32[32]{0:T(128)} %constant.25) | copy-start | bytes 388
  80.5 172.0 %reduce-scatter.11.cloned.1.call-start = ((), (), s32[]{:S(2)}) async-start(), calls=%async_computation.7 | async-start | bytes 294912 | tf_op jit(solution)/shard_map/reduce_scatter | solution.py:74
Sparse Core Ops, SparseCore 0:
  15.7 43.8 all-gather.1
  75.1 23.9 reduce-scatter.12
  101.7 21.6 reduce-scatter.8
  126.6 61.9 reduce-scatter.6
  192.1 60.2 reduce-scatter.10
where the time goes:
time: 261 us; the launch traced here: 260 us
  waiting for transfers between devices  144 us (55%)
  blocking collectives  69.6 us (27%)
  matrix products  15.8 us (6%)
  between operations  14.6 us (6%)
  local copies, waits for them, and re-layouts  8.91 us (3%)
  other arithmetic  6.99 us (3%)
    reduce_scatter x1, waiting for transfers between devices, body(): lax.psum_scatter(subject_grad.astype(jnp.bfloat16), 'obj', scatter_dimens...  62.6 us
    reduce_scatter x1, waiting for transfers between devices, body(): lax.psum_scatter(partial_rows, 'obj', scatter_dimension=2, tiled=True)  62.4 us
    all_gather x1, blocking collectives, body(): subject_block = lax.all_gather(subject_factors, 'obj', axis=0, tiled=True)  32.6 us
    unnamed x1, blocking collectives  21.4 us
    unnamed x6, waiting for transfers between devices  18.6 us
    all_gather x1, blocking collectives, body(): row_pieces = lax.all_gather(relations, 'subj', axis=1, tiled=True)  8.36 us
    all_gather x1, blocking collectives, body(): object_block = lax.all_gather(object_factors, 'subj', axis=0, tiled=True)  7.29 us
    unnamed x27, local copies, waits for them, and re-layouts  7.19 us
  transfers between devices with their start and end apart: 5, of which 4 were waited for; matrix products, arithmetic and copies ran while one was open for 6% of the time, Pallas kernels for 0%

commit v1 on v0

v1 whole, which is shorter than its diff:
```python
import functools

import jax
import jax.numpy as jnp
from jax import lax
from jax.experimental import pallas as pl
from jax.experimental.pallas import tpu as pltpu
from jax.sharding import PartitionSpec as P

F32 = jnp.float32
BF16 = jnp.bfloat16
PAIR = 2
LANES = 128
CHUNK = 128


def mm(a, b, ca, cb):
    return lax.dot_general(a, b, (((ca,), (cb,)), ((), ())), preferred_element_type=F32)


def kernel(
    nx, nh, copies,
    s_hbm, o_hbm, r_in, lab_hbm,
    gs_out, go_out, gr_out, loss_out,
    s_all, o_all, r_own, r_all, r_full, labels, left, right, resid, carried,
    gsub, gr, gr_crx, gr_tx, gr_xrx, gr_ytx, gr_yrx, gr_ztx, gr_zrx,
    go, go_crx, go_tx, go_xrx, gs, gs_yrx, gs_ztx, gs_zrx,
    send_sem, recv_sem, local_sem,
):
    subj = lax.axis_index("subj")
    obj = lax.axis_index("obj")
    x, c = subj // PAIR, subj % PAIR
    z, y = obj // PAIR, obj % PAIR
    oc, oy = 1 - c, 1 - y
    rels, rank = r_full.shape[0], r_full.shape[1]
    rows_r, wid = r_in.shape[1], r_in.shape[2]
    rows_s = s_all.shape[2]
    ns = nh * PAIR * rows_s
    no = nx * PAIR * o_all.shape[2]
    core_dev = (x * PAIR + oc, obj)
    y_dev = (subj, z * PAIR + oy)

    def xs(e):
        return lax.rem(x + e, nx)

    def zs(d):
        return lax.rem(z + d, nh)

    def x_from(e):
        return lax.rem(x - e + nx, nx)

    def z_from(d):
        return lax.rem(z - d + nh, nh)

    def x_dev(e):
        return (xs(e) * PAIR + c, obj)

    def z_dev(d):
        return (subj, zs(d) * PAIR + y)

    started = []

    def send(src, dst, dev):
        i = len(started)
        cp = pltpu.make_async_remote_copy(
            src_ref=src, dst_ref=dst, send_sem=send_sem.at[i], recv_sem=recv_sem.at[i],
            device_id=dev, device_id_type=pl.DeviceIdType.MESH,
        )
        cp.start()
        started.append(cp)
        return cp

    lab_cp = pltpu.make_async_copy(lab_hbm, labels, local_sem.at[0])
    lab_cp.start()
    s_cp = pltpu.make_async_copy(s_hbm, s_all.at[z, y], local_sem.at[1])
    s_cp.start()
    o_cp = pltpu.make_async_copy(o_hbm, o_all.at[x, c], local_sem.at[2])
    o_cp.start()
    for k in range(rels):
        r_own[:, k * wid:(k + 1) * wid] = r_in[k]
    r_cp = pltpu.make_async_copy(r_own, r_all.at[z, y, x, c], local_sem.at[3])
    r_cp.start()

    barrier = pltpu.get_barrier_semaphore()
    partners = [core_dev, y_dev] + [x_dev(e) for e in range(1, nx)] + [z_dev(d) for d in range(1, nh)]
    for dev in partners:
        pl.semaphore_signal(barrier, inc=1, device_id=dev, device_id_type=pl.DeviceIdType.MESH)
    pl.semaphore_wait(barrier, len(partners))

    order = [d for d in range(nh)]
    rz, sz = {}, {}
    for d in range(1, nh):
        rz[d] = send(r_own, r_all.at[z, y, x, c], z_dev(d))
    for d in range(1, nh):
        sz[d] = send(s_hbm, s_all.at[z, y], z_dev(d))
    ox = {e: send(o_hbm, o_all.at[x, c], x_dev(e)) for e in range(1, nx)}
    ocr = {0: send(o_hbm, o_all.at[x, c], core_dev)}
    ry, sy = {}, {}
    ry[0] = send(r_own, r_all.at[z, y, x, c], y_dev)
    sy[0] = send(s_hbm, s_all.at[z, y], y_dev)
    r_cp.wait()
    rx, rc = {}, {}

    def spread(d):
        blk = r_all.at[z_from(d), :, x, c]
        for e in range(1, nx):
            rx[d, e] = send(blk, blk, x_dev(e))
        rc[d, 0] = send(blk, blk, core_dev)

    for d in order[1:]:
        rz[d].wait_recv()
        blk = r_all.at[z_from(d), y, x, c]
        ry[d] = send(blk, blk, y_dev)
    for d in order:
        ry[d].wait_recv()
        spread(d)
    for e in range(1, nx):
        ox[e].wait_recv()
        blk = o_all.at[x_from(e), c]
        ocr[e] = send(blk, blk, core_dev)
    for d in order[1:]:
        sz[d].wait_recv()
        blk = s_all.at[z_from(d), y]
        sy[d] = send(blk, blk, y_dev)
    for d in order:
        for e in range(1, nx):
            rx[d, e].wait_recv()
            blk = r_all.at[z_from(d), :, x_from(e), c]
            rc[d, e] = send(blk, blk, core_dev)
    for key in rc:
        rc[key].wait_recv()
    for o in range(nh * PAIR):
        v = r_all[o // PAIR, o % PAIR].reshape(rank, rels * wid)
        for k in range(rels):
            r_full[k, :, o * wid:(o + 1) * wid] = v[:, k * wid:(k + 1) * wid]
    s_cp.wait()
    for d in order:
        sy[d].wait_recv()
    s_blk = s_all[...].reshape(ns, rank)
    for k in range(rels):
        left[k] = mm(s_blk, r_full[k], 1, 0).astype(BF16)
    o_cp.wait()
    for e in range(nx):
        ocr[e].wait_recv()
    lab_cp.wait()

    gsub[:, rank:] = jnp.zeros((ns, LANES), F32)
    for k in range(rels):
        def rows_body(i, carry, k=k):
            r = pl.ds(pl.multiple_of(i * CHUNK, CHUNK), CHUNK)
            ob = o_all[...].reshape(no, rank)
            sc = mm(left[k, r, :], ob, 1, 1)
            codes = labels[k, r, :]
            edge = codes == 2
            target = jnp.where(edge, 1.0, 0.0).astype(F32)
            weight = jnp.where(codes > 0, 1.0, 0.0).astype(F32)
            e = jnp.exp(-jnp.abs(sc))
            inv = 1.0 / (1.0 + e)
            sig = jnp.where(sc >= 0, inv, e * inv)
            soft = jnp.maximum(sc, 0.0) + jnp.log1p(e)
            cell = weight * (soft - target * sc)
            gsub[r, rank:] += jnp.broadcast_to(
                jnp.sum(cell, axis=1, keepdims=True), (CHUNK, LANES))
            res = (weight * (sig - target)).astype(BF16)
            resid[k, r, :] = res
            carried[k, r, :] = mm(res, ob, 1, 0).astype(BF16)
            return carry
        lax.fori_loop(0, ns // CHUNK, rows_body, 0)
        term = mm(s_all[...].reshape(ns, rank), carried[k], 0, 0).astype(BF16)
        for o in range(nh * PAIR):
            gr[o % PAIR, o // PAIR, :, :, :, k * wid:(k + 1) * wid] = (
                term[:, o * wid:(o + 1) * wid].reshape(nx, PAIR, rows_r, wid))

    grc = {}
    for e in list(range(1, nx)) + [0]:
        grc[e] = send(gr.at[:, :, xs(e), oc], gr_crx.at[e], core_dev)

    acc = mm(resid[0], left[0], 0, 0)
    for k in range(1, rels):
        acc = acc + mm(resid[k], left[k], 0, 0)
    go[...] = acc.astype(BF16).reshape(go.shape)
    goc = {}
    for e in list(range(1, nx)) + [0]:
        goc[e] = send(go.at[xs(e), oc], go_crx.at[e], core_dev)

    grx = {}
    for e in range(1, nx):
        grc[e].wait_recv()
        for first in (1, 0):
            q = oy if first else y
            gr_tx[e, q] = (gr[q, :, xs(e), c].astype(F32) + gr_crx[e, q].astype(F32)).astype(BF16)
            grx[e, first] = send(gr_tx.at[e, q], gr_xrx.at[e, q], x_dev(e))

    ob = o_all[...].reshape(no, rank)
    for k in range(rels):
        right[k] = mm(ob, r_full[k], 1, 1).astype(BF16)
    acc = mm(resid[0], right[0], 1, 0)
    for k in range(1, rels):
        acc = acc + mm(resid[k], right[k], 1, 0)
    objects = no * nh * PAIR
    gs[:, :, :, :rank] = acc.astype(BF16).reshape(nh, PAIR, rows_s, rank)
    gs[:, :, :, rank:] = (gsub[:, rank:] / (rels * objects)).astype(BF16).reshape(nh, PAIR, rows_s, LANES)
    gsy = {}
    for d in order[1:] + [0]:
        gsy[d] = send(gs.at[zs(d), oy], gs_yrx.at[d], y_dev)

    gox = {}
    for e in range(1, nx):
        goc[e].wait_recv()
        go_tx[e] = (go[xs(e), c].astype(F32) + go_crx[e].astype(F32)).astype(BF16)
        gox[e] = send(go_tx.at[e], go_xrx.at[e], x_dev(e))

    grc[0].wait_recv()
    for e in range(1, nx):
        grx[e, 1].wait_recv()
    t = gr[oy, :, x, c].astype(F32) + gr_crx[0, oy].astype(F32)
    for e in range(1, nx):
        t = t + gr_xrx[e, oy].astype(F32)
    gr_ytx[...] = t.astype(BF16)
    gry = send(gr_ytx, gr_yrx, y_dev)

    gsz = {}
    for d in order[1:]:
        gsy[d].wait_recv()
        gs_ztx[d] = (gs[zs(d), y].astype(F32) + gs_yrx[d].astype(F32)).astype(BF16)
        gsz[d] = send(gs_ztx.at[d], gs_zrx.at[d], z_dev(d))

    for e in range(1, nx):
        grx[e, 0].wait_recv()
    gry.wait_recv()

    def gr_sum(zz):
        t = gr[y, zz, x, c].astype(F32) + gr_crx[0, y, zz].astype(F32)
        for e in range(1, nx):
            t = t + gr_xrx[e, y, zz].astype(F32)
        return t + gr_yrx[zz].astype(F32)

    grz = {}
    for d in order[1:]:
        gr_ztx[d] = gr_sum(zs(d)).astype(BF16)
        grz[d] = send(gr_ztx.at[d], gr_zrx.at[d], z_dev(d))

    goc[0].wait_recv()
    t = go[x, c].astype(F32) + go_crx[0].astype(F32)
    for e in range(1, nx):
        gox[e].wait_recv()
        t = t + go_xrx[e].astype(F32)
    go_out[...] = t
    gsy[0].wait_recv()
    t = gs[z, y].astype(F32) + gs_yrx[0].astype(F32)
    for d in order[1:]:
        gsz[d].wait_recv()
        t = t + gs_zrx[d].astype(F32)
    gs_out[...] = t[:, :rank]
    loss_out[...] = t[:, rank:]
    t = gr_sum(z)
    for d in order[1:]:
        grz[d].wait_recv()
        t = t + gr_zrx[d].astype(F32)
    t = t / (ns * nx * PAIR)
    for k in range(rels):
        gr_out[k] = t[:, k * wid:(k + 1) * wid]
    for cp in started:
        cp.wait_send()


def body(subject_factors, object_factors, relations, labels):
    n_subj, n_obj = lax.axis_size("subj"), lax.axis_size("obj")
    nx, nh = n_subj // PAIR, n_obj // PAIR
    rows_s, rank = subject_factors.shape
    rows_o = object_factors.shape[0]
    rels, rows_r, wid = relations.shape
    pack = rels * wid
    ns, no = rows_s * n_obj, rows_o * n_subj
    copies = 64 + 4 * nh + 8 * nx + 3 * nh * nx
    v = pltpu.VMEM
    scratch = [
        v((nh, PAIR, rows_s, rank), BF16),
        v((nx, PAIR, rows_o, rank), BF16),
        v((rows_r, pack), BF16),
        v((nh, PAIR, nx, PAIR, rows_r, pack), BF16),
        v((rels, rank, rank), BF16),
        v(labels.shape, jnp.int32),
        v((rels, ns, rank), BF16),
        v((rels, no, rank), BF16),
        v((rels, ns, no), BF16),
        v((rels, ns, rank), BF16),
        v((ns, rank + LANES), F32),
        v((PAIR, nh, nx, PAIR, rows_r, pack), BF16),
        v((nx, PAIR, nh, rows_r, pack), BF16),
        v((nx, PAIR, nh, rows_r, pack), BF16),
        v((nx, PAIR, nh, rows_r, pack), BF16),
        v((nh, rows_r, pack), BF16),
        v((nh, rows_r, pack), BF16),
        v((nh, rows_r, pack), BF16),
        v((nh, rows_r, pack), BF16),
        v((nx, PAIR, rows_o, rank), BF16),
        v((nx, rows_o, rank), BF16),
        v((nx, rows_o, rank), BF16),
        v((nx, rows_o, rank), BF16),
        v((nh, PAIR, rows_s, rank + LANES), BF16),
        v((nh, rows_s, rank + LANES), BF16),
        v((nh, rows_s, rank + LANES), BF16),
        v((nh, rows_s, rank + LANES), BF16),
        pltpu.SemaphoreType.DMA((copies,)),
        pltpu.SemaphoreType.DMA((copies,)),
        pltpu.SemaphoreType.DMA((4,)),
    ]
    hbm = pl.BlockSpec(memory_space=pl.ANY)
    vm = pl.BlockSpec(memory_space=pltpu.VMEM)
    grad_subject, grad_object, grad_relations, loss = pl.pallas_call(
        functools.partial(kernel, nx, nh, copies),
        out_shape=(
            jax.ShapeDtypeStruct((rows_s, rank), F32),
            jax.ShapeDtypeStruct((rows_o, rank), F32),
            jax.ShapeDtypeStruct((rels, rows_r, wid), F32),
            jax.ShapeDtypeStruct((rows_s, LANES), F32),
        ),
        in_specs=[hbm, hbm, vm, hbm],
        out_specs=(vm, vm, vm, vm),
        scratch_shapes=scratch,
        compiler_params=pltpu.CompilerParams(
            collective_id=0, has_side_effects=True, vmem_limit_bytes=48 * 1024 * 1024
        ),
    )(subject_factors, object_factors, relations, labels)
    return grad_subject, grad_object, grad_relations, loss[:, 0]


def solution(mesh):
    placed = (
        P(("subj", "obj"), None),
        P(("obj", "subj"), None),
        P(None, "subj", "obj"),
        P(None, "subj", "obj"),
    )
    return jax.shard_map(
        body,
        mesh=mesh,
        in_specs=placed,
        out_specs=(
            P(("subj", "obj"), None),
            P(("obj", "subj"), None),
            P(None, "subj", "obj"),
            P(("subj", "obj")),
        ),
        check_vma=False,
    )
```

time: 261 us -> 56.8 us (0.22)
  waiting for transfers between devices: 144 us -> 0 us
  blocking collectives: 69.6 us -> 0 us
  Pallas kernels: 0 us -> 49 us
  matrix products: 15.8 us -> 0 us
  between operations: 14.6 us -> 0.65 us
  other arithmetic: 6.99 us -> 0 us
    reduce_scatter x3 -> x0, waiting for transfers between devices: 125 us -> none  [the longest x1 62.6 us: body(): lax.psum_scatter(subject_grad.astype(jnp.bfloat16), 'obj', scatter_dimens...]
    pallas_call x0 -> x1, Pallas kernels: none -> 49 us  [body(): pl.pallas_call(functools.partial(kernel, nx, nh, copies), out_shape=(jax....]
    all_gather x3 -> x0, blocking collectives: 48.2 us -> none  [the longest x1 32.6 us: body(): subject_block = lax.all_gather(subject_factors, 'obj', axis=0, tiled=True)]
    unnamed x1 -> x0, blocking collectives: 21.4 us -> none
    unnamed x6 -> x0, waiting for transfers between devices: 18.6 us -> none
    dot_general x10 -> x0, matrix products: 15.8 us -> none  [the longest x2 4.35 us: body(): jnp.einsum('ic,ia->ca', subject_block, carried, preferred_element_type=jn...]
    convert_element_type x6 -> x0, other arithmetic: 4.46 us -> none  [the longest x2 2.09 us: body(): grad_subject, loss_rows = (lax.psum_scatter(subject_grad.astype(jnp.bfloa...]
    unnamed x27 -> x10, local copies, waits for them, and re-layouts: 7.19 us -> 6.27 us
  transfers between devices with their start and end apart: 5 -> 0, of which waited for: 4 -> 0; matrix products, arithmetic and copies ran while one was open for 6% -> 0% of each run, Pallas kernels for 0% -> 0%
where the time goes in v1:
time: 56.8 us; the launch traced here: 56.6 us
  Pallas kernels  49 us (86%)
  local copies, waits for them, and re-layouts  6.9 us (12%)
  between operations  0.65 us (1%)
    pallas_call x1, Pallas kernels, body(): pl.pallas_call(functools.partial(kernel, nx, nh, copies), out_shape=(jax....  49 us
    unnamed x10, local copies, waits for them, and re-layouts  6.27 us

profile of v1, /device:TPU:0, one launch (start us, length us, event | category | flops | bytes accessed | tf_op | source)
XLA Modules:
  0.0 56.6 jit_solution(14816475593091047438)
XLA Ops:
  0.6 0.9 %copy.10.r_in = bf16[2,128,64]{2,1,0:T(8,128)(2,1)S(1)} copy(bf16[2,128,64]{1,2,0:T(8,128)(2,1)} %param.6) | data formatting | bytes 65536 | tf_op args[2]
  1.5 0.0 copy-start
  1.5 1.6 %copy-done = s32[2,512,512]{2,1,0:T(8,128)S(1)} copy-done((s32[2,512,512]{2,1,0:T(8,128)S(1)}, s32[2,512,512]{2,1,0:T(8,128)}, u32[]{:S(2)}) %copy-start) | copy-done | bytes 2097176
  3.1 0.0 copy-start.1
  3.1 0.9 %copy-done.1 = bf16[128,512]{1,0:T(8,128)(2,1)S(1)} copy-done((bf16[128,512]{1,0:T(8,128)(2,1)S(1)}, bf16[128,512]{1,0:T(8,128)(2,1)}, u32[]{:S(2)}) %copy-start.1) | copy-done | bytes 131096
  4.0 0.0 copy-start.2
  4.0 0.8 %copy-done.2 = bf16[64,512]{1,0:T(8,128)(2,1)S(1)} copy-done((bf16[64,512]{1,0:T(8,128)(2,1)S(1)}, bf16[64,512]{1,0:T(8,128)(2,1)}, u32[]{:S(2)}) %copy-start.2) | copy-done | bytes 65560
  4.8 49.0 %shard_map.75 = (f32[64,512]{1,0:T(8,128)S(1)}, f32[128,512]{1,0:T(8,128)S(1)}, f32[2,128,64]{2,1,0:T(8,128)S(1)}, f32[64,128]{1,0:T(8,128)S(1)}) custom-call(bf16[64,512]{1,0:T(8,128)(2,1)S(1)} %copy-done.2, bf16[128,512]{1,0:T(8,128)(2,1)S(1)} %copy-done.1, bf16[2,128,64]{2,1,0:T(8,128)(2,1)S(1)} %copy.10.r_in, s32[2,512,512]{2,1,0:T(8,128)S(1)} %copy-done), custom_call_target="tpu_custom_call" | custom-call | tf_op jit(solution)/shard_map/pallas_call | solution.py:311
  53.9 0.6 %slice_reduce_fusion = f32[64]{0:T(128)} fusion(f32[64,128]{1,0:T(8,128)S(1)} %get-tuple-element.11), kind=kLoop, calls=%fused_computation | loop fusion | bytes 512 | tf_op jit(solution)/shard_map/slice | solution.py:326
  54.5 0.7 %copy.11 = f32[2,128,64]{1,2,0:T(8,128)} copy(f32[2,128,64]{2,1,0:T(8,128)S(1)} %get-tuple-element.18) | data formatting | bytes 131072
  55.2 0.7 %copy.14 = f32[64,512]{1,0:T(8,128)} copy(f32[64,512]{1,0:T(8,128)S(1)} %get-tuple-element.24) | data formatting | bytes 262144
  55.9 0.7 %copy.15 = f32[128,512]{1,0:T(8,128)} copy(f32[128,512]{1,0:T(8,128)S(1)} %get-tuple-element.25) | data formatting | bytes 524288
Async XLA Ops:
  1.5 1.6 %copy-start = (s32[2,512,512]{2,1,0:T(8,128)S(1)}, s32[2,512,512]{2,1,0:T(8,128)}, u32[]{:S(2)}) copy-start(s32[2,512,512]{2,1,0:T(8,128)} %lab_hbm.1) | copy-start | bytes 6291460
  3.1 0.9 %copy-start.1 = (bf16[128,512]{1,0:T(8,128)(2,1)S(1)}, bf16[128,512]{1,0:T(8,128)(2,1)}, u32[]{:S(2)}) copy-start(bf16[128,512]{1,0:T(8,128)(2,1)} %o_hbm.1) | copy-start | bytes 393220
  4.0 0.8 %copy-start.2 = (bf16[64,512]{1,0:T(8,128)(2,1)S(1)}, bf16[64,512]{1,0:T(8,128)(2,1)}, u32[]{:S(2)}) copy-start(bf16[64,512]{1,0:T(8,128)(2,1)} %s_hbm.1) | copy-start | bytes 196612

commit v2 on v1

v2 whole, which is shorter than its diff:
```python
import functools

import jax
import jax.numpy as jnp
from jax import lax
from jax.experimental import pallas as pl
from jax.experimental.pallas import tpu as pltpu
from jax.sharding import PartitionSpec as P

F32 = jnp.float32
BF16 = jnp.bfloat16
PAIR = 2
LANES = 128
CHUNK = 64


def mm(a, b, ca, cb):
    return lax.dot_general(a, b, (((ca,), (cb,)), ((), ())), preferred_element_type=F32)


def kernel(
    nx, nh,
    s_hbm, o_hbm, r_hbm, lab_hbm,
    gs_out, go_out, gr_out,
    s_all, o_all, r_all, r_full, labels, left, right, score, resid, carried,
    loss, gr, gr_crx, gr_tx, gr_xrx, gr_ytx, gr_yrx, gr_ztx, gr_zrx,
    go, go_crx, go_tx, go_xrx, gs, gs_yrx, gs_ztx, gs_zrx,
    send_sem, recv_sem, local_sem,
):
    subj = lax.axis_index("subj")
    obj = lax.axis_index("obj")
    x, c = subj // PAIR, subj % PAIR
    z, y = obj // PAIR, obj % PAIR
    oc, oy = 1 - c, 1 - y
    rels, rank = r_full.shape[0], r_full.shape[1]
    wid, rows_r = r_hbm.shape[1], r_hbm.shape[2]
    rows_s = s_all.shape[2]
    ns = nh * PAIR * rows_s
    no = nx * PAIR * o_all.shape[2]
    core_dev = (x * PAIR + oc, obj)
    y_dev = (subj, z * PAIR + oy)

    def xs(e):
        return lax.rem(x + e, nx)

    def zs(d):
        return lax.rem(z + d, nh)

    def x_from(e):
        return lax.rem(x - e + nx, nx)

    def z_from(d):
        return lax.rem(z - d + nh, nh)

    def x_dev(e):
        return (xs(e) * PAIR + c, obj)

    def z_dev(d):
        return (subj, zs(d) * PAIR + y)

    started = []

    def send(src, dst, dev):
        i = len(started)
        cp = pltpu.make_async_remote_copy(
            src_ref=src, dst_ref=dst, send_sem=send_sem.at[i], recv_sem=recv_sem.at[i],
            device_id=dev, device_id_type=pl.DeviceIdType.MESH,
        )
        cp.start()
        started.append(cp)
        return cp

    barrier = pltpu.get_barrier_semaphore()
    partners = [core_dev, y_dev] + [x_dev(e) for e in range(1, nx)] + [z_dev(d) for d in range(1, nh)]
    for dev in partners:
        pl.semaphore_signal(barrier, inc=1, device_id=dev, device_id_type=pl.DeviceIdType.MESH)

    r_cp = pltpu.make_async_copy(r_hbm, r_all.at[z, y, x, c], local_sem.at[3])
    r_cp.start()
    s_cp = pltpu.make_async_copy(s_hbm, s_all.at[z, y], local_sem.at[1])
    s_cp.start()
    o_cp = pltpu.make_async_copy(o_hbm, o_all.at[x, c], local_sem.at[2])
    o_cp.start()
    lab_cp = pltpu.make_async_copy(lab_hbm, labels, local_sem.at[0])
    lab_cp.start()
    loss[...] = jnp.zeros_like(loss)
    pl.semaphore_wait(barrier, len(partners))

    order = [d for d in range(nh)]
    rz, sz = {}, {}
    for d in range(1, nh):
        rz[d] = send(r_hbm, r_all.at[z, y, x, c], z_dev(d))
    ry, sy = {}, {}
    ry[0] = send(r_hbm, r_all.at[z, y, x, c], y_dev)
    ox = {e: send(o_hbm, o_all.at[x, c], x_dev(e)) for e in range(1, nx)}
    ocr = {0: send(o_hbm, o_all.at[x, c], core_dev)}
    for d in range(1, nh):
        sz[d] = send(s_hbm, s_all.at[z, y], z_dev(d))
    sy[0] = send(s_hbm, s_all.at[z, y], y_dev)
    r_cp.wait()
    rx, rc = {}, {}

    def spread(d):
        ry[d].wait_recv()
        blk = r_all.at[z_from(d), :, x, c]
        for e in range(1, nx):
            rx[d, e] = send(blk, blk, x_dev(e))
        rc[d, 0] = send(blk, blk, core_dev)

    for d in order:
        if d:
            rz[d].wait_recv()
            blk = r_all.at[z_from(d), y, x, c]
            ry[d] = send(blk, blk, y_dev)
        if d != 1:
            spread(d - 1 if d else 0)
    if nh > 1:
        spread(nh - 1)
    for e in range(1, nx):
        ox[e].wait_recv()
        blk = o_all.at[x_from(e), c]
        ocr[e] = send(blk, blk, core_dev)
    for d in order[1:]:
        sz[d].wait_recv()
        blk = s_all.at[z_from(d), y]
        sy[d] = send(blk, blk, y_dev)
    for d in order:
        for e in range(1, nx):
            rx[d, e].wait_recv()
            blk = r_all.at[z_from(d), :, x_from(e), c]
            rc[d, e] = send(blk, blk, core_dev)
    for key in rc:
        rc[key].wait_recv()
    for s in range(nx * PAIR):
        for k in range(rels):
            r_full[k, :, s * rows_r:(s + 1) * rows_r] = (
                r_all[:, :, s // PAIR, s % PAIR, k].reshape(rank, rows_r))
    s_cp.wait()
    for d in order:
        sy[d].wait_recv()
    for k in range(rels):
        left[k] = mm(s_all[...].reshape(ns, rank), r_full[k], 1, 1).astype(BF16)
    o_cp.wait()
    for e in range(nx):
        ocr[e].wait_recv()
    score[...] = mm(
        left[...].reshape(rels * ns, rank), o_all[...].reshape(no, rank), 1, 1
    ).reshape(rels, ns, no)
    lab_cp.wait()

    for k in range(rels):
        def rows_body(i, carry, k=k):
            r = pl.ds(pl.multiple_of(i * CHUNK, CHUNK), CHUNK)
            sc = score[k, r, :]
            codes = labels[k, r, :]
            target = jnp.where(codes == 2, 1.0, 0.0).astype(F32)
            held = codes > 0
            e = jnp.exp(-jnp.abs(sc))
            inv = 1.0 / (1.0 + e)
            sig = jnp.where(sc >= 0, inv, e * inv)
            soft = jnp.maximum(sc, 0.0) + jnp.log1p(e)
            cell = jnp.where(held, soft - target * sc, 0.0)
            part = loss[r, :]
            for g in range(no // LANES):
                part = part + cell[:, g * LANES:(g + 1) * LANES]
            loss[r, :] = part
            resid[k, r, :] = jnp.where(held, sig - target, 0.0).astype(BF16)
            return carry
        lax.fori_loop(0, ns // CHUNK, rows_body, 0)

    carried[...] = mm(
        resid[...].reshape(rels * ns, no), o_all[...].reshape(no, rank), 1, 0
    ).astype(BF16).reshape(rels, ns, rank)
    for k in range(rels):
        term = mm(carried[k], s_all[...].reshape(ns, rank), 0, 0).astype(BF16)
        for s in range(nx * PAIR):
            gr[:, :, s // PAIR, s % PAIR, k] = (
                term[:, s * rows_r:(s + 1) * rows_r].reshape(nh, PAIR, wid, rows_r))
    grc = {}
    for e in list(range(1, nx)) + [0]:
        grc[e] = send(gr.at[:, :, xs(e), oc], gr_crx.at[e], core_dev)

    acc = None
    for k in range(rels):
        right[k] = mm(o_all[...].reshape(no, rank), r_full[k], 1, 0).astype(BF16)
        t = mm(resid[k], right[k], 1, 0)
        acc = t if acc is None else acc + t
    objects = no * nh * PAIR
    gs[:, :, :, :rank] = acc.astype(BF16).reshape(nh, PAIR, rows_s, rank)
    row_loss = jnp.sum(loss[...], axis=1, keepdims=True) / (rels * objects)
    gs[:, :, :, rank:] = jnp.broadcast_to(row_loss, (ns, LANES)).astype(BF16).reshape(
        nh, PAIR, rows_s, LANES)
    gsy = {}
    for d in order[1:] + [0]:
        gsy[d] = send(gs.at[zs(d), oy], gs_yrx.at[d], y_dev)

    grx = {}
    for e in range(1, nx):
        grc[e].wait_recv()
        for first in (1, 0):
            q = oy if first else y
            gr_tx[e, q] = (gr[:, q, xs(e), c].astype(F32) + gr_crx[e, :, q].astype(F32)).astype(BF16)
            grx[e, first] = send(gr_tx.at[e, q], gr_xrx.at[e, q], x_dev(e))

    acc = None
    for k in range(rels):
        t = mm(resid[k], left[k], 0, 0)
        acc = t if acc is None else acc + t
    go[...] = acc.astype(BF16).reshape(go.shape)
    goc = {}
    for e in list(range(1, nx)) + [0]:
        goc[e] = send(go.at[xs(e), oc], go_crx.at[e], core_dev)

    def gr_sum(d, q):
        t = gr[zs(d), q, x, c].astype(F32) + gr_crx[0, zs(d), q].astype(F32)
        for e in range(1, nx):
            t = t + gr_xrx[e, q, zs(d)].astype(F32)
        return t

    gox = {}
    for e in range(1, nx):
        goc[e].wait_recv()
        go_tx[e] = (go[xs(e), c].astype(F32) + go_crx[e].astype(F32)).astype(BF16)
        gox[e] = send(go_tx.at[e], go_xrx.at[e], x_dev(e))

    grc[0].wait_recv()
    for e in range(1, nx):
        grx[e, 1].wait_recv()
    gry = {}
    for d in order[1:] + [0]:
        gr_ytx[d] = gr_sum(d, oy).astype(BF16)
        gry[d] = send(gr_ytx.at[d], gr_yrx.at[d], y_dev)

    gsz = {}
    for d in order[1:]:
        gsy[d].wait_recv()
        gs_ztx[d] = (gs[zs(d), y].astype(F32) + gs_yrx[d].astype(F32)).astype(BF16)
        gsz[d] = send(gs_ztx.at[d], gs_zrx.at[d], z_dev(d))

    for e in range(1, nx):
        grx[e, 0].wait_recv()
    grz = {}
    for d in order[1:]:
        gry[d].wait_recv()
        gr_ztx[d] = (gr_sum(d, y) + gr_yrx[d].astype(F32)).astype(BF16)
        grz[d] = send(gr_ztx.at[d], gr_zrx.at[d], z_dev(d))

    goc[0].wait_recv()
    t = go[x, c].astype(F32) + go_crx[0].astype(F32)
    for e in range(1, nx):
        gox[e].wait_recv()
        t = t + go_xrx[e].astype(F32)
    go_out[...] = t
    gsy[0].wait_recv()
    t = gs[z, y].astype(F32) + gs_yrx[0].astype(F32)
    for d in order[1:]:
        gsz[d].wait_recv()
        t = t + gs_zrx[d].astype(F32)
    gs_out[...] = t
    gry[0].wait_recv()
    t = gr_sum(0, y) + gr_yrx[0].astype(F32)
    for d in order[1:]:
        grz[d].wait_recv()
        t = t + gr_zrx[d].astype(F32)
    gr_out[...] = t / (ns * nx * PAIR)
    for cp in started:
        cp.wait_send()


def finish(gs_in, go_in, gr_in, gs_out, go_out, gr_out, loss_out):
    rank = gs_out.shape[1]
    gs_out[...] = gs_in[:, :rank]
    go_out[...] = go_in[...]
    gr_out[...] = gr_in[...]
    loss_out[...] = gs_in[:, rank:].T[0:1, :]


def body(subject_factors, object_factors, relations, labels):
    n_subj, n_obj = lax.axis_size("subj"), lax.axis_size("obj")
    nx, nh = n_subj // PAIR, n_obj // PAIR
    rows_s, rank = subject_factors.shape
    rows_o = object_factors.shape[0]
    rels, rows_r, wid = relations.shape
    ns, no = rows_s * n_obj, rows_o * n_subj
    copies = (nh * (4 + 2 * nx) + 2 * nx) + (3 * nh + 2 * nx + 2 * nx + 2 * nx + 2 * nh)
    v = pltpu.VMEM
    piece = (rels, wid, rows_r)
    scratch = [
        v((nh, PAIR, rows_s, rank), BF16),
        v((nx, PAIR, rows_o, rank), BF16),
        v((nh, PAIR, nx, PAIR) + piece, BF16),
        v((rels, rank, rank), BF16),
        v(labels.shape, jnp.int32),
        v((rels, ns, rank), BF16),
        v((rels, no, rank), BF16),
        v((rels, ns, no), F32),
        v((rels, ns, no), BF16),
        v((rels, ns, rank), BF16),
        v((ns, LANES), F32),
        v((nh, PAIR, nx, PAIR) + piece, BF16),
        v((nx, nh, PAIR) + piece, BF16),
        v((nx, PAIR, nh) + piece, BF16),
        v((nx, PAIR, nh) + piece, BF16),
        v((nh,) + piece, BF16),
        v((nh,) + piece, BF16),
        v((nh,) + piece, BF16),
        v((nh,) + piece, BF16),
        v((nx, PAIR, rows_o, rank), BF16),
        v((nx, rows_o, rank), BF16),
        v((nx, rows_o, rank), BF16),
        v((nx, rows_o, rank), BF16),
        v((nh, PAIR, rows_s, rank + LANES), BF16),
        v((nh, rows_s, rank + LANES), BF16),
        v((nh, rows_s, rank + LANES), BF16),
        v((nh, rows_s, rank + LANES), BF16),
        pltpu.SemaphoreType.DMA((copies,)),
        pltpu.SemaphoreType.DMA((copies,)),
        pltpu.SemaphoreType.DMA((4,)),
    ]
    hbm = pl.BlockSpec(memory_space=pl.ANY)
    vm = pl.BlockSpec(memory_space=pltpu.VMEM)
    sums = pl.pallas_call(
        functools.partial(kernel, nx, nh),
        out_shape=(
            jax.ShapeDtypeStruct((rows_s, rank + LANES), F32),
            jax.ShapeDtypeStruct((rows_o, rank), F32),
            jax.ShapeDtypeStruct(piece, F32),
        ),
        in_specs=[hbm, hbm, hbm, hbm],
        out_specs=(vm, vm, vm),
        scratch_shapes=scratch,
        compiler_params=pltpu.CompilerParams(
            collective_id=0, has_side_effects=True, vmem_limit_bytes=63 * 1024 * 1024
        ),
    )(subject_factors, object_factors, jnp.swapaxes(relations, 1, 2), labels)
    grad_subject, grad_object, grad_relations, loss = pl.pallas_call(
        finish,
        out_shape=(
            jax.ShapeDtypeStruct((rows_s, rank), F32),
            jax.ShapeDtypeStruct((rows_o, rank), F32),
            jax.ShapeDtypeStruct(piece, F32),
            jax.ShapeDtypeStruct((1, rows_s), F32),
        ),
        in_specs=[vm, vm, vm],
        out_specs=(vm, vm, vm, vm),
        compiler_params=pltpu.CompilerParams(vmem_limit_bytes=63 * 1024 * 1024),
    )(*sums)
    return grad_subject, grad_object, jnp.swapaxes(grad_relations, 1, 2), loss.reshape(rows_s)


def solution(mesh):
    placed = (
        P(("subj", "obj"), None),
        P(("obj", "subj"), None),
        P(None, "subj", "obj"),
        P(None, "subj", "obj"),
    )
    return jax.shard_map(
        body,
        mesh=mesh,
        in_specs=placed,
        out_specs=(
            P(("subj", "obj"), None),
            P(("obj", "subj"), None),
            P(None, "subj", "obj"),
            P(("subj", "obj")),
        ),
        check_vma=False,
    )
```

time: 56.8 us -> 48.1 us (0.85)
  local copies, waits for them, and re-layouts: 6.9 us -> 0 us
  Pallas kernels: 49 us -> 47.3 us
    unnamed x10 -> x0, local copies, waits for them, and re-layouts: 6.27 us -> none
    pallas_call x1 -> x2, Pallas kernels: 49 us -> 47.3 us  [the longest x1 45.5 us: body(): pl.pallas_call(functools.partial(kernel, nx, nh), out_shape=(jax.ShapeDty...]
    slice x1 -> x0, local copies, waits for them, and re-layouts: 0.63 us -> none  [body(): return (grad_subject, grad_object, grad_relations, loss[:, 0])]
where the time goes in v2:
time: 48.1 us; the launch traced here: 48 us
  Pallas kernels  47.3 us (98%)
  between operations  0.64 us (1%)
    pallas_call x1, Pallas kernels, body(): pl.pallas_call(functools.partial(kernel, nx, nh), out_shape=(jax.ShapeDty...  45.5 us
    pallas_call x1, Pallas kernels, body(): pl.pallas_call(finish, out_shape=(jax.ShapeDtypeStruct((rows_s, rank), F3...  1.78 us

profile of v2, /device:TPU:0, one launch (start us, length us, event | category | flops | bytes accessed | tf_op | source)
XLA Modules:
  0.0 48.0 jit_solution(10968773237629437547)
XLA Ops:
  0.6 45.5 %shard_map.75 = (f32[64,640]{1,0:T(8,128)}, f32[128,512]{1,0:T(8,128)}, f32[2,64,128]{2,1,0:T(8,128)}) custom-call(bf16[64,512]{1,0:T(8,128)(2,1)} %s_hbm.1, bf16[128,512]{1,0:T(8,128)(2,1)} %o_hbm.1, bf16[2,64,128]{2,1,0:T(8,128)(2,1)} %bitcast.3, s32[2,512,512]{2,1,0:T(8,128)} %lab_hbm.1), custom_call_target="tpu_custom_call" | custom-call | tf_op jit(solution)/shard_map/pallas_call | solution.py:322
  46.2 1.8 %shard_map.76 = (f32[64,512]{1,0:T(8,128)}, f32[128,512]{1,0:T(8,128)}, f32[2,64,128]{2,1,0:T(8,128)}, f32[1,64]{1,0:T(1,128)}) custom-call(f32[64,640]{1,0:T(8,128)} %get-tuple-element.11.gs_in, f32[128,512]{1,0:T(8,128)} %get-tuple-element.12.go_in, f32[2,64,128]{2,1,0:T(8,128)} %get-tuple-element.13.gr_in), custom_call_target="tpu_custom_call" | custom-call | tf_op jit(solution)/shard_map/pallas_call | solution.py:336

commit v3 on v2

--- a/solution.py
+++ b/solution.py
@@ -11,6 +11,7 @@
 BF16 = jnp.bfloat16
 PAIR = 2
 LANES = 128
+TILE = 16
 CHUNK = 64
 
 
@@ -21,10 +22,11 @@
 def kernel(
     nx, nh,
     s_hbm, o_hbm, r_hbm, lab_hbm,
-    gs_out, go_out, gr_out,
-    s_all, o_all, r_all, r_full, labels, left, right, score, resid, carried,
+    gs_out, go_out, gr_out, loss_out,
+    s_all, o_all, r_all, r_full, labels, left, right, score, resid,
     loss, gr, gr_crx, gr_tx, gr_xrx, gr_ytx, gr_yrx, gr_ztx, gr_zrx,
     go, go_crx, go_tx, go_xrx, gs, gs_yrx, gs_ztx, gs_zrx,
+    ls, ls_yrx, ls_ztx, ls_zrx,
     send_sem, recv_sem, local_sem,
 ):
     subj = lax.axis_index("subj")
@@ -84,6 +86,7 @@
     lab_cp = pltpu.make_async_copy(lab_hbm, labels, local_sem.at[0])
     lab_cp.start()
     loss[...] = jnp.zeros_like(loss)
+    ls[...] = jnp.zeros_like(ls)
     pl.semaphore_wait(barrier, len(partners))
 
     order = [d for d in range(nh)]
@@ -120,38 +123,49 @@
         ox[e].wait_recv()
         blk = o_all.at[x_from(e), c]
         ocr[e] = send(blk, blk, core_dev)
-    for d in order[1:]:
-        sz[d].wait_recv()
-        blk = s_all.at[z_from(d), y]
-        sy[d] = send(blk, blk, y_dev)
     for d in order:
         for e in range(1, nx):
             rx[d, e].wait_recv()
             blk = r_all.at[z_from(d), :, x_from(e), c]
             rc[d, e] = send(blk, blk, core_dev)
+        if d:
+            sz[d].wait_recv()
+            blk = s_all.at[z_from(d), y]
+            sy[d] = send(blk, blk, y_dev)
     for key in rc:
         rc[key].wait_recv()
     for s in range(nx * PAIR):
         for k in range(rels):
             r_full[k, :, s * rows_r:(s + 1) * rows_r] = (
                 r_all[:, :, s // PAIR, s % PAIR, k].reshape(rank, rows_r))
+    o_cp.wait()
+    for e in range(nx):
+        ocr[e].wait_recv()
+    for k in range(rels):
+        right[k] = mm(o_all[...].reshape(no, rank), r_full[k], 1, 0).astype(BF16)
     s_cp.wait()
     for d in order:
         sy[d].wait_recv()
+    lab_cp.wait()
+    turns = list(range(1, nx)) + [0]
+    grc, grx = {}, {}
+
+    def gr_along_x(k):
+        for e in range(1, nx):
+            grc[k, e].wait_recv()
+            for first in (1, 0):
+                q = oy if first else y
+                gr_tx[e, q, k] = (
+                    gr[k, :, q, xs(e), c].astype(F32) + gr_crx[k, e, :, q].astype(F32)).astype(BF16)
+                grx[k, e, first] = send(gr_tx.at[e, q, k], gr_xrx.at[e, q, k], x_dev(e))
+
     for k in range(rels):
         left[k] = mm(s_all[...].reshape(ns, rank), r_full[k], 1, 1).astype(BF16)
-    o_cp.wait()
-    for e in range(nx):
-        ocr[e].wait_recv()
-    score[...] = mm(
-        left[...].reshape(rels * ns, rank), o_all[...].reshape(no, rank), 1, 1
-    ).reshape(rels, ns, no)
-    lab_cp.wait()
-
-    for k in range(rels):
+        score[...] = mm(left[k], o_all[...].reshape(no, rank), 1, 1)
+
         def rows_body(i, carry, k=k):
             r = pl.ds(pl.multiple_of(i * CHUNK, CHUNK), CHUNK)
-            sc = score[k, r, :]
+            sc = score[r, :]
             codes = labels[k, r, :]
             target = jnp.where(codes == 2, 1.0, 0.0).astype(F32)
             held = codes > 0
@@ -167,40 +181,31 @@
             resid[k, r, :] = jnp.where(held, sig - target, 0.0).astype(BF16)
             return carry
         lax.fori_loop(0, ns // CHUNK, rows_body, 0)
-
-    carried[...] = mm(
-        resid[...].reshape(rels * ns, no), o_all[...].reshape(no, rank), 1, 0
-    ).astype(BF16).reshape(rels, ns, rank)
-    for k in range(rels):
-        term = mm(carried[k], s_all[...].reshape(ns, rank), 0, 0).astype(BF16)
+        carried = mm(resid[k], o_all[...].reshape(no, rank), 1, 0).astype(BF16)
+        term = mm(carried, s_all[...].reshape(ns, rank), 0, 0).astype(BF16)
         for s in range(nx * PAIR):
-            gr[:, :, s // PAIR, s % PAIR, k] = (
+            gr[k, :, :, s // PAIR, s % PAIR] = (
                 term[:, s * rows_r:(s + 1) * rows_r].reshape(nh, PAIR, wid, rows_r))
-    grc = {}
-    for e in list(range(1, nx)) + [0]:
-        grc[e] = send(gr.at[:, :, xs(e), oc], gr_crx.at[e], core_dev)
+        for e in turns:
+            grc[k, e] = send(gr.at[k, :, :, xs(e), oc], gr_crx.at[k, e], core_dev)
+        if k:
+            gr_along_x(k - 1)
 
     acc = None
     for k in range(rels):
-        right[k] = mm(o_all[...].reshape(no, rank), r_full[k], 1, 0).astype(BF16)
         t = mm(resid[k], right[k], 1, 0)
         acc = t if acc is None else acc + t
     objects = no * nh * PAIR
-    gs[:, :, :, :rank] = acc.astype(BF16).reshape(nh, PAIR, rows_s, rank)
-    row_loss = jnp.sum(loss[...], axis=1, keepdims=True) / (rels * objects)
-    gs[:, :, :, rank:] = jnp.broadcast_to(row_loss, (ns, LANES)).astype(BF16).reshape(
-        nh, PAIR, rows_s, LANES)
+    gs[...] = acc.astype(BF16).reshape(nh, PAIR, rows_s, rank)
     gsy = {}
     for d in order[1:] + [0]:
         gsy[d] = send(gs.at[zs(d), oy], gs_yrx.at[d], y_dev)
-
-    grx = {}
-    for e in range(1, nx):
-        grc[e].wait_recv()
-        for first in (1, 0):
-            q = oy if first else y
-            gr_tx[e, q] = (gr[:, q, xs(e), c].astype(F32) + gr_crx[e, :, q].astype(F32)).astype(BF16)
-            grx[e, first] = send(gr_tx.at[e, q], gr_xrx.at[e, q], x_dev(e))
+    gr_along_x(rels - 1)
+    row_loss = jnp.sum(loss[...].T, axis=0, keepdims=True) / (rels * objects)
+    for o in range(nh * PAIR):
+        ls[o % PAIR, o // PAIR, :, :rows_s] = jnp.broadcast_to(
+            row_loss[:, o * rows_s:(o + 1) * rows_s], (TILE, rows_s)).astype(BF16)
+    lsy = send(ls.at[oy], ls_yrx, y_dev)
 
     acc = None
     for k in range(rels):
@@ -208,13 +213,13 @@
         acc = t if acc is None else acc + t
     go[...] = acc.astype(BF16).reshape(go.shape)
     goc = {}
-    for e in list(range(1, nx)) + [0]:
+    for e in turns:
         goc[e] = send(go.at[xs(e), oc], go_crx.at[e], core_dev)
 
     def gr_sum(d, q):
-        t = gr[zs(d), q, x, c].astype(F32) + gr_crx[0, zs(d), q].astype(F32)
-        for e in range(1, nx):
-            t = t + gr_xrx[e, q, zs(d)].astype(F32)
+        t = gr[:, zs(d), q, x, c].astype(F32) + gr_crx[:, 0, zs(d), q].astype(F32)
+        for e in range(1, nx):
+            t = t + gr_xrx[e, q, :, zs(d)].astype(F32)
         return t
 
     gox = {}
@@ -223,9 +228,10 @@
         go_tx[e] = (go[xs(e), c].astype(F32) + go_crx[e].astype(F32)).astype(BF16)
         gox[e] = send(go_tx.at[e], go_xrx.at[e], x_dev(e))
 
-    grc[0].wait_recv()
-    for e in range(1, nx):
-        grx[e, 1].wait_recv()
+    for k in range(rels):
+        grc[k, 0].wait_recv()
+        for e in range(1, nx):
+            grx[k, e, 1].wait_recv()
     gry = {}
     for d in order[1:] + [0]:
         gr_ytx[d] = gr_sum(d, oy).astype(BF16)
@@ -237,8 +243,15 @@
         gs_ztx[d] = (gs[zs(d), y].astype(F32) + gs_yrx[d].astype(F32)).astype(BF16)
         gsz[d] = send(gs_ztx.at[d], gs_zrx.at[d], z_dev(d))
 
-    for e in range(1, nx):
-        grx[e, 0].wait_recv()
+    lsy.wait_recv()
+    lsz = {}
+    for d in order[1:]:
+        ls_ztx[d] = (ls[y, zs(d)].astype(F32) + ls_yrx[zs(d)].astype(F32)).astype(BF16)
+        lsz[d] = send(ls_ztx.at[d], ls_zrx.at[d], z_dev(d))
+
+    for k in range(rels):
+        for e in range(1, nx):
+            grx[k, e, 0].wait_recv()
     grz = {}
     for d in order[1:]:
         gry[d].wait_recv()
@@ -257,6 +270,11 @@
         gsz[d].wait_recv()
         t = t + gs_zrx[d].astype(F32)
     gs_out[...] = t
+    t = ls[y, z].astype(F32) + ls_yrx[z].astype(F32)
+    for d in order[1:]:
+        lsz[d].wait_recv()
+        t = t + ls_zrx[d].astype(F32)
+    loss_out[...] = t[0:1, :rows_s]
     gry[0].wait_recv()
     t = gr_sum(0, y) + gr_yrx[0].astype(F32)
     for d in order[1:]:
@@ -267,12 +285,14 @@
         cp.wait_send()
 
 
-def finish(gs_in, go_in, gr_in, gs_out, go_out, gr_out, loss_out):
-    rank = gs_out.shape[1]
-    gs_out[...] = gs_in[:, :rank]
-    go_out[...] = go_in[...]
-    gr_out[...] = gr_in[...]
-    loss_out[...] = gs_in[:, rank:].T[0:1, :]
+def finish(*refs):
+    count = len(refs) // 2
+    sem = refs[-1]
+    moves = [pltpu.make_async_copy(refs[i], refs[count + i], sem.at[i]) for i in range(count)]
+    for m in moves:
+        m.start()
+    for m in moves:
+        m.wait()
 
 
 def body(subject_factors, object_factors, relations, labels):
@@ -282,7 +302,8 @@
     rows_o = object_factors.shape[0]
     rels, rows_r, wid = relations.shape
     ns, no = rows_s * n_obj, rows_o * n_subj
-    copies = (nh * (4 + 2 * nx) + 2 * nx) + (3 * nh + 2 * nx + 2 * nx + 2 * nx + 2 * nh)
+    copies = nh * (4 + 2 * nx) + 2 * nx + 5 * nh + 2 * nx + rels * 3 * nx + nh
+    lw = -(-rows_s // LANES) * LANES
     v = pltpu.VMEM
     piece = (rels, wid, rows_r)
     scratch = [
@@ -293,14 +314,13 @@
         v(labels.shape, jnp.int32),
         v((rels, ns, rank), BF16),
         v((rels, no, rank), BF16),
-        v((rels, ns, no), F32),
+        v((ns, no), F32),
         v((rels, ns, no), BF16),
-        v((rels, ns, rank), BF16),
         v((ns, LANES), F32),
-        v((nh, PAIR, nx, PAIR) + piece, BF16),
-        v((nx, nh, PAIR) + piece, BF16),
-        v((nx, PAIR, nh) + piece, BF16),
-        v((nx, PAIR, nh) + piece, BF16),
+        v((rels, nh, PAIR, nx, PAIR, wid, rows_r), BF16),
+        v((rels, nx, nh, PAIR, wid, rows_r), BF16),
+        v((nx, PAIR, rels, nh, wid, rows_r), BF16),
+        v((nx, PAIR, rels, nh, wid, rows_r), BF16),
         v((nh,) + piece, BF16),
         v((nh,) + piece, BF16),
         v((nh,) + piece, BF16),
@@ -309,25 +329,31 @@
         v((nx, rows_o, rank), BF16),
         v((nx, rows_o, rank), BF16),
         v((nx, rows_o, rank), BF16),
-        v((nh, PAIR, rows_s, rank + LANES), BF16),
-        v((nh, rows_s, rank + LANES), BF16),
-        v((nh, rows_s, rank + LANES), BF16),
-        v((nh, rows_s, rank + LANES), BF16),
+        v((nh, PAIR, rows_s, rank), BF16),
+        v((nh, rows_s, rank), BF16),
+        v((nh, rows_s, rank), BF16),
+        v((nh, rows_s, rank), BF16),
+        v((PAIR, nh, TILE, lw), BF16),
+        v((nh, TILE, lw), BF16),
+        v((nh, TILE, lw), BF16),
+        v((nh, TILE, lw), BF16),
         pltpu.SemaphoreType.DMA((copies,)),
         pltpu.SemaphoreType.DMA((copies,)),
         pltpu.SemaphoreType.DMA((4,)),
     ]
     hbm = pl.BlockSpec(memory_space=pl.ANY)
     vm = pl.BlockSpec(memory_space=pltpu.VMEM)
+    results = (
+        jax.ShapeDtypeStruct((rows_s, rank), F32),
+        jax.ShapeDtypeStruct((rows_o, rank), F32),
+        jax.ShapeDtypeStruct(piece, F32),
+        jax.ShapeDtypeStruct((1, rows_s), F32),
+    )
     sums = pl.pallas_call(
         functools.partial(kernel, nx, nh),
-        out_shape=(
-            jax.ShapeDtypeStruct((rows_s, rank + LANES), F32),
-            jax.ShapeDtypeStruct((rows_o, rank), F32),
-            jax.ShapeDtypeStruct(piece, F32),
-        ),
+        out_shape=results,
         in_specs=[hbm, hbm, hbm, hbm],
-        out_specs=(vm, vm, vm),
+        out_specs=(vm, vm, vm, vm),
         scratch_shapes=scratch,
         compiler_params=pltpu.CompilerParams(
             collective_id=0, has_side_effects=True, vmem_limit_bytes=63 * 1024 * 1024
@@ -335,14 +361,10 @@
     )(subject_factors, object_factors, jnp.swapaxes(relations, 1, 2), labels)
     grad_subject, grad_object, grad_relations, loss = pl.pallas_call(
         finish,
-        out_shape=(
-            jax.ShapeDtypeStruct((rows_s, rank), F32),
-            jax.ShapeDtypeStruct((rows_o, rank), F32),
-            jax.ShapeDtypeStruct(piece, F32),
-            jax.ShapeDtypeStruct((1, rows_s), F32),
-        ),
-        in_specs=[vm, vm, vm],
-        out_specs=(vm, vm, vm, vm),
+        out_shape=results,
+        in_specs=[hbm] * 4,
+        out_specs=(hbm,) * 4,
+        scratch_shapes=[pltpu.SemaphoreType.DMA((4,))],
         compiler_params=pltpu.CompilerParams(vmem_limit_bytes=63 * 1024 * 1024),
     )(*sums)
     return grad_subject, grad_object, jnp.swapaxes(grad_relations, 1, 2), loss.reshape(rows_s)

time: 48.1 us -> 61.1 us (1.27)
  Pallas kernels: 47.3 us -> 60.3 us
    pallas_call x2, Pallas kernels: 47.3 us -> 60.3 us  [the longest x1 45.3 us: body(): pl.pallas_call(functools.partial(kernel, nx, nh), out_shape=results, in_s...]
where the time goes in v3:
time: 61.1 us; the launch traced here: 61 us
  Pallas kernels  60.3 us (99%)
  between operations  0.64 us (1%)
    pallas_call x1, Pallas kernels, body(): pl.pallas_call(functools.partial(kernel, nx, nh), out_shape=results, in_s...  45.3 us
    pallas_call x1, Pallas kernels, body(): pl.pallas_call(finish, out_shape=results, in_specs=[hbm] * 4, out_specs=(...  15.1 us

profile of v3, /device:TPU:0, one launch (start us, length us, event | category | flops | bytes accessed | tf_op | source)
XLA Modules:
  0.0 61.0 jit_solution(16393906501143508930)
XLA Ops:
  0.6 45.3 %shard_map.75 = (f32[64,512]{1,0:T(8,128)}, f32[128,512]{1,0:T(8,128)}, f32[2,64,128]{2,1,0:T(8,128)}, f32[1,64]{1,0:T(1,128)}) custom-call(bf16[64,512]{1,0:T(8,128)(2,1)} %s_hbm.1, bf16[128,512]{1,0:T(8,128)(2,1)} %o_hbm.1, bf16[2,64,128]{2,1,0:T(8,128)(2,1)} %bitcast.3, s32[2,512,512]{2,1,0:T(8,128)} %lab_hbm.1), custom_call_target="tpu_custom_call" | custom-call | tf_op jit(solution)/shard_map/pallas_call | solution.py:352
  45.9 15.1 %shard_map.76 = (f32[64,512]{1,0:T(8,128)}, f32[128,512]{1,0:T(8,128)}, f32[2,64,128]{2,1,0:T(8,128)}, f32[1,64]{1,0:T(1,128)}) custom-call(f32[64,512]{1,0:T(8,128)} %get-tuple-element.12.refs_0_, f32[128,512]{1,0:T(8,128)} %get-tuple-element.13.refs_1_, f32[2,64,128]{2,1,0:T(8,128)} %get-tuple-element.14.refs_2_, f32[1,64]{1,0:T(1,128)} %get-tuple-element.15.refs_3_), custom_call_target="tpu_custom_call" | custom-call | tf_op jit(solution)/shard_map/pallas_call | solution.py:362

commit v4 on v3

--- a/solution.py
+++ b/solution.py
@@ -90,17 +90,20 @@
     pl.semaphore_wait(barrier, len(partners))
 
     order = [d for d in range(nh)]
+    r_mine, s_mine, o_mine = r_all.at[z, y, x, c], s_all.at[z, y], o_all.at[x, c]
+    r_cp.wait()
     rz, sz = {}, {}
     for d in range(1, nh):
-        rz[d] = send(r_hbm, r_all.at[z, y, x, c], z_dev(d))
+        rz[d] = send(r_mine, r_mine, z_dev(d))
     ry, sy = {}, {}
-    ry[0] = send(r_hbm, r_all.at[z, y, x, c], y_dev)
-    ox = {e: send(o_hbm, o_all.at[x, c], x_dev(e)) for e in range(1, nx)}
-    ocr = {0: send(o_hbm, o_all.at[x, c], core_dev)}
+    ry[0] = send(r_mine, r_mine, y_dev)
+    o_cp.wait()
+    ox = {e: send(o_mine, o_mine, x_dev(e)) for e in range(1, nx)}
+    ocr = {0: send(o_mine, o_mine, core_dev)}
+    s_cp.wait()
     for d in range(1, nh):
-        sz[d] = send(s_hbm, s_all.at[z, y], z_dev(d))
-    sy[0] = send(s_hbm, s_all.at[z, y], y_dev)
-    r_cp.wait()
+        sz[d] = send(s_mine, s_mine, z_dev(d))
+    sy[0] = send(s_mine, s_mine, y_dev)
     rx, rc = {}, {}
 
     def spread(d):
@@ -138,12 +141,10 @@
         for k in range(rels):
             r_full[k, :, s * rows_r:(s + 1) * rows_r] = (
                 r_all[:, :, s // PAIR, s % PAIR, k].reshape(rank, rows_r))
-    o_cp.wait()
     for e in range(nx):
         ocr[e].wait_recv()
     for k in range(rels):
         right[k] = mm(o_all[...].reshape(no, rank), r_full[k], 1, 0).astype(BF16)
-    s_cp.wait()
     for d in order:
         sy[d].wait_recv()
     lab_cp.wait()
@@ -170,9 +171,9 @@
             target = jnp.where(codes == 2, 1.0, 0.0).astype(F32)
             held = codes > 0
             e = jnp.exp(-jnp.abs(sc))
-            inv = 1.0 / (1.0 + e)
-            sig = jnp.where(sc >= 0, inv, e * inv)
-            soft = jnp.maximum(sc, 0.0) + jnp.log1p(e)
+            tail = jnp.where(e < 2.0 ** -8, e - 0.5 * e * e, jnp.log(1.0 + e))
+            sig = jnp.exp(jnp.minimum(sc, 0.0) - tail)
+            soft = jnp.maximum(sc, 0.0) + tail
             cell = jnp.where(held, soft - target * sc, 0.0)
             part = loss[r, :]
             for g in range(no // LANES):
@@ -285,14 +286,11 @@
         cp.wait_send()
 
 
-def finish(*refs):
-    count = len(refs) // 2
-    sem = refs[-1]
-    moves = [pltpu.make_async_copy(refs[i], refs[count + i], sem.at[i]) for i in range(count)]
-    for m in moves:
-        m.start()
-    for m in moves:
-        m.wait()
+def finish(gs_in, go_in, gr_in, loss_in, gs_out, go_out, gr_out, loss_out):
+    gs_out[...] = gs_in[...]
+    go_out[...] = go_in[...]
+    gr_out[...] = gr_in[...]
+    loss_out[...] = loss_in[...]
 
 
 def body(subject_factors, object_factors, relations, labels):
@@ -362,9 +360,8 @@
     grad_subject, grad_object, grad_relations, loss = pl.pallas_call(
         finish,
         out_shape=results,
-        in_specs=[hbm] * 4,
-        out_specs=(hbm,) * 4,
-        scratch_shapes=[pltpu.SemaphoreType.DMA((4,))],
+        in_specs=[vm] * 4,
+        out_specs=(vm,) * 4,
         compiler_params=pltpu.CompilerParams(vmem_limit_bytes=63 * 1024 * 1024),
     )(*sums)
     return grad_subject, grad_object, jnp.swapaxes(grad_relations, 1, 2), loss.reshape(rows_s)

time: 61.1 us -> 47.5 us (0.78)
  Pallas kernels: 60.3 us -> 46.7 us
    pallas_call x1, Pallas kernels: 15.1 us -> 1.77 us  [body(): pl.pallas_call(finish, out_shape=results, in_specs=[vm] * 4, out_specs=(v...]
where the time goes in v4:
time: 47.5 us; the launch traced here: 47.3 us
  Pallas kernels  46.7 us (98%)
  between operations  0.64 us (1%)
    pallas_call x1, Pallas kernels, body(): pl.pallas_call(functools.partial(kernel, nx, nh), out_shape=results, in_s...  44.9 us
    pallas_call x1, Pallas kernels, body(): pl.pallas_call(finish, out_shape=results, in_specs=[vm] * 4, out_specs=(v...  1.77 us

profile of v4, /device:TPU:0, one launch (start us, length us, event | category | flops | bytes accessed | tf_op | source)
XLA Modules:
  0.0 47.3 jit_solution(6629521359705040684)
XLA Ops:
  0.6 44.9 %shard_map.75 = (f32[64,512]{1,0:T(8,128)}, f32[128,512]{1,0:T(8,128)}, f32[2,64,128]{2,1,0:T(8,128)}, f32[1,64]{1,0:T(1,128)}) custom-call(bf16[64,512]{1,0:T(8,128)(2,1)} %s_hbm.1, bf16[128,512]{1,0:T(8,128)(2,1)} %o_hbm.1, bf16[2,64,128]{2,1,0:T(8,128)(2,1)} %bitcast.3, s32[2,512,512]{2,1,0:T(8,128)} %lab_hbm.1), custom_call_target="tpu_custom_call" | custom-call | tf_op jit(solution)/shard_map/pallas_call | solution.py:350
  45.6 1.8 %shard_map.76 = (f32[64,512]{1,0:T(8,128)}, f32[128,512]{1,0:T(8,128)}, f32[2,64,128]{2,1,0:T(8,128)}, f32[1,64]{1,0:T(1,128)}) custom-call(f32[64,512]{1,0:T(8,128)} %get-tuple-element.12.gs_in, f32[128,512]{1,0:T(8,128)} %get-tuple-element.13.go_in, f32[2,64,128]{2,1,0:T(8,128)} %get-tuple-element.14.gr_in, f32[1,64]{1,0:T(1,128)} %get-tuple-element.15.loss_in), custom_call_target="tpu_custom_call" | custom-call | tf_op jit(solution)/shard_map/pallas_call | solution.py:360
